TPU v7x, 32 devices: a whole 2x2x4 slice. The times are simulated.
32 devices in a mesh: dp: 4 (over y, core), context: 8 (over z, x).
Axes of the slice: x: 2, y: 2, z: 4, core: 2. Of those that a mesh axis runs over, the one named last changes fastest.
Arguments:
- queries: bfloat16 [4, 1024, 2048], P('dp', 'context'), may hold values from -6 to 6
- keys: bfloat16 [4, 1024, 2048], P('dp', 'context'), may hold values from -6 to 6
- values: bfloat16 [4, 1024, 2048], P('dp', 'context'), may hold values from -6 to 6
- out_grad: bfloat16 [4, 1024, 2048], P('dp', 'context'), may hold values from -6 to 6
- log_gates: float32 [4, 16, 1024], P('dp', None, 'context'), may hold values from -1 to 0, as said below
- query_map: bfloat16 [16, 128, 128], replicated, may hold values from -0.5 to 0.5
- key_map: bfloat16 [16, 128, 128], replicated, may hold values from -0.5 to 0.5
Outputs:
- query_grad: bfloat16 [4, 1024, 2048], P('dp', 'context')
- key_grad: bfloat16 [4, 1024, 2048], P('dp', 'context')
- value_grad: bfloat16 [4, 1024, 2048], P('dp', 'context')
- map_grads: float32 [4096, 128], P(('dp', 'context'))
Inputs may be any that keep to these rules, and one draw needn't show every extreme that they name: `log_gates`: every entry is negative.
All inputs are finite; a program needn't handle non-finite values.
Results may differ from a plain program's by a relative error of at most 0.019.
Values may be sent and summed in bfloat16 or wider, within the bound.
A program may use at most 128 MiB of HBM per device.

v0:
```python
import jax
import jax.numpy as jnp
from jax import lax
from jax.sharding import PartitionSpec as P

split_mode = lax.Precision.HIGH


def carried_in(value, axis, combine, identity, reverse):
    devices, mine = (lax.axis_size(axis), lax.axis_index(axis))
    everything = jax.tree.map(lambda part: lax.all_gather(part, axis), value)
    start = jax.tree.map(
        lambda part, zero: jnp.broadcast_to(jnp.asarray(zero, part.dtype), part.shape),
        value,
        identity,
    )

    def hop(k, before):
        at = devices - 1 - k if reverse else k
        reached = at > mine if reverse else at < mine
        new = combine(before, jax.tree.map(lambda part: part[at], everything))
        return jax.tree.map(lambda a, b: jnp.where(reached, a, b), new, before)

    return lax.fori_loop(0, devices, hop, start)


def decay_tables(gates):
    running = jnp.cumsum(gates, axis=2)
    closing = running[:, :, -1]
    length = gates.shape[2]
    causal = jnp.arange(length)[:, None] >= jnp.arange(length)[None, :]
    spread = running[:, :, :, None] - running[:, :, None, :]
    within = jnp.where(causal, jnp.exp(jnp.where(causal, spread, 0.0)), 0.0)
    to_end = jnp.exp(closing[:, :, None] - running)
    from_start = jnp.exp(running)
    return (within, to_end, from_start, closing)


def chain(earlier, later):
    later_log = later[0].astype(jnp.float32)
    factor = jnp.exp(later_log)[:, :, None, None]
    total = factor * earlier[1].astype(jnp.float32) + later[1].astype(jnp.float32)
    joined_log = earlier[0].astype(jnp.float32) + later_log
    return (joined_log.astype(jnp.bfloat16), total.astype(jnp.bfloat16))


def per_device(queries, keys, values, out_grad, log_gates, query_map, key_map):
    heads, width = (query_map.shape[0], query_map.shape[1])
    batch, length = (queries.shape[0], queries.shape[1])
    shape = (batch, length, heads, width)
    key_scale = width ** (-0.5) / 16.0
    query_heads = queries.reshape(shape)
    key_heads = keys.reshape(shape)
    value_heads = values.reshape(shape)
    grad_heads = out_grad.reshape(shape)
    feat_query = jnp.einsum(
        "btha,had->bthd", query_heads, query_map, preferred_element_type=jnp.float32
    ).astype(jnp.bfloat16)
    feat_key = (
        jnp.einsum("btha,had->bthd", key_heads, key_map, preferred_element_type=jnp.float32)
        * key_scale
    ).astype(jnp.bfloat16)
    within, to_end, from_start, closing = decay_tables(log_gates)
    closing_log = closing.astype(jnp.bfloat16)
    scores = (
        jnp.einsum("bthd,bshd->bhts", feat_query, feat_key, preferred_element_type=jnp.float32)
        * within
    ).astype(jnp.bfloat16)
    grad_scores = (
        jnp.einsum("bthd,bshd->bhts", grad_heads, value_heads, preferred_element_type=jnp.float32)
        * within
    ).astype(jnp.bfloat16)
    start_weight = jnp.transpose(from_start, (0, 2, 1))[..., None]
    end_weight = jnp.transpose(to_end, (0, 2, 1))[..., None]
    key_weighted = feat_key * end_weight
    query_weighted = feat_query * start_weight
    states_local = jnp.einsum(
        "bshi,bshj->bhij",
        key_weighted,
        value_heads,
        precision=split_mode,
        preferred_element_type=jnp.float32,
    ).astype(jnp.bfloat16)
    grads_local = jnp.einsum(
        "bthi,bthj->bhij",
        query_weighted,
        grad_heads,
        precision=split_mode,
        preferred_element_type=jnp.float32,
    ).astype(jnp.bfloat16)
    identity = (jnp.zeros_like(closing_log), jnp.zeros_like(states_local))
    state_in = carried_in((closing_log, states_local), "context", chain, identity, False)[1]
    grad_in = carried_in((closing_log, grads_local), "context", chain, identity, True)[1]
    query_total = (
        jnp.einsum("bhts,bshd->bthd", grad_scores, feat_key, preferred_element_type=jnp.float32)
        + jnp.einsum("bthj,bhij->bthi", grad_heads, state_in, preferred_element_type=jnp.float32)
        * start_weight
    )
    key_total = (
        jnp.einsum("bhts,bthd->bshd", grad_scores, feat_query, preferred_element_type=jnp.float32)
        + jnp.einsum("bshj,bhij->bshi", value_heads, grad_in, preferred_element_type=jnp.float32)
        * end_weight
    )
    value_total = (
        jnp.einsum("bhts,bthd->bshd", scores, grad_heads, preferred_element_type=jnp.float32)
        + jnp.einsum("bshi,bhij->bshj", feat_key, grad_in, preferred_element_type=jnp.float32)
        * end_weight
    )
    query_back = query_total.astype(jnp.bfloat16)
    key_back = (key_total * key_scale).astype(jnp.bfloat16)
    query_grad = (
        jnp.einsum("bthd,had->btha", query_back, query_map, preferred_element_type=jnp.float32)
        .astype(jnp.bfloat16)
        .reshape(batch, length, heads * width)
    )
    key_grad = (
        jnp.einsum("bthd,had->btha", key_back, key_map, preferred_element_type=jnp.float32)
        .astype(jnp.bfloat16)
        .reshape(batch, length, heads * width)
    )
    value_grad = value_total.astype(jnp.bfloat16).reshape(batch, length, heads * width)
    total_tokens = batch * lax.axis_size("dp") * length * lax.axis_size("context")
    partial_sums = jnp.stack(
        [
            jnp.einsum(
                "btha,bthd->had", query_heads, query_back, preferred_element_type=jnp.float32
            ),
            jnp.einsum("btha,bthd->had", key_heads, key_back, preferred_element_type=jnp.float32),
        ]
    ).reshape(2 * heads * width, width) * total_tokens ** (-0.5)
    by_group = lax.psum_scatter(
        partial_sums.astype(jnp.bfloat16), "dp", scatter_dimension=0, tiled=True
    )
    map_grads = lax.psum_scatter(by_group, "context", scatter_dimension=0, tiled=True).astype(
        jnp.float32
    )
    return (query_grad, key_grad, value_grad, map_grads)


def solution(mesh):
    return jax.shard_map(
        per_device,
        mesh=mesh,
        in_specs=(
            P("dp", "context", None),
            P("dp", "context", None),
            P("dp", "context", None),
            P("dp", "context", None),
            P("dp", None, "context"),
            P(),
            P(),
        ),
        out_specs=(
            P("dp", "context", None),
            P("dp", "context", None),
            P("dp", "context", None),
            P(("dp", "context"), None),
        ),
        check_vma=False,
    )
```

profile of v0, /device:TPU:0, one launch (start us, length us, event | category | flops | bytes accessed | tf_op | source)
XLA Modules:
  0.0 274.8 jit_solution(1554196347803569740)
XLA Ops:
  7.2 0.0 copy-start
  7.2 0.0 all-gather.6.cloned.1.call-start
  7.2 1.1 reduce_window_sum.11
  8.3 0.1 slice.4
  8.4 0.1 copy.131
  8.5 0.1 exponential_bitcast_fusion.2
  8.5 1.3 copy.132
  9.9 1.3 copy.135
  11.3 0.4 fusion.15
  11.6 0.4 copy-done.4
  12.0 1.3 convolution_convert_fusion.4
  13.3 0.0 all-gather.6.cloned.1.call-update
  13.3 0.0 all-gather.8.cloned.1.call-start
  13.4 0.3 copy.133
  13.7 0.3 copy.134
  14.0 0.4 convolution_convert_fusion.2
  14.3 1.6 convolution_convert_fusion.3
  16.0 0.0 all-gather.8.cloned.1.call-update
  16.0 0.0 reduce-scatter.3.cloned.1.call-start
  16.1 22.3 %all-gather = bf16[8,16,1]{1,2,0:T(2,128)(2,1)S(1)} all-gather(bf16[1,16,1]{1,2,0:T(2,128)(2,1)S(1)} %convert_element_type.205), channel_id=2, replica_groups=mesh['dp'=4,'context'=8] {'context'}, dimensions={0}, use_global_device_ids=true | all-gather | bytes 288 | tf_op jit(solution)/shard_map/all_gather | solution.py:11
  38.4 2.4 fusion.16
  40.8 48.8 %all-gather.6.cloned.1.call-done = bf16[128,128,128]{2,1,0:T(8,128)(2,1)} async-done(((bf16[16,128,128]{2,1,0:T(8,128)(2,1)}), bf16[128,128,128]{2,1,0:T(8,128)(2,1)}) %all-gather.6.cloned.1.call-update) | async-done | bytes 4194320 | tf_op jit(solution)/shard_map/all_gather | solution.py:11
  89.6 11.7 %while.30 = (s32[]{:T(128)}, bf16[1,16,128,128]{3,2,1,0:T(8,128)(2,1)S(1)}, s32[]{:T(128)}, bf16[8,1,16]{2,1,0:T(2,128)(2,1)S(1)}, bf16[8,1,16,128,128]{4,3,2,1,0:T(8,128)(2,1)}, /*index=5*/s32[]{:T(128)}, s32[]{:T(128)}) while((s32[]{:T(128)}, bf16[1,16,128,128]{3,2,1,0:T(8,128)(2,1)S(1)}, s32[]{:T(128)}, ...), condition=%wide.region_2.3_spmd.clone, body=%wide.region_1.2_spmd.clone.sunk | while | flops 1835028 | bytes 1573129 | solution.py:24
  89.6 1.4 fusion.68
  91.1 1.4 fusion.68
  92.5 1.4 fusion.68
  94.0 1.4 fusion.68
  95.4 1.4 fusion.68
  96.9 1.5 fusion.68
  98.4 1.5 fusion.68
  99.9 1.4 fusion.68
  101.3 0.3 fusion.6
  101.6 0.7 copy-done.11
  102.4 0.5 fusion.18
  102.8 1.5 convolution_bitcast_fusion.2
  104.3 59.1 %all-gather.8.cloned.1.call-done = bf16[128,128,128]{2,1,0:T(8,128)(2,1)} async-done(((bf16[16,128,128]{2,1,0:T(8,128)(2,1)}), bf16[128,128,128]{2,1,0:T(8,128)(2,1)}) %all-gather.8.cloned.1.call-update) | async-done | bytes 4194320 | tf_op jit(solution)/shard_map/all_gather | solution.py:11
  163.4 11.8 %while.31 = (s32[]{:T(128)}, bf16[1,16,128,128]{3,2,1,0:T(8,128)(2,1)S(1)}, s32[]{:T(128)}, bf16[8,1,16]{2,1,0:T(2,128)(2,1)S(1)}, bf16[8,1,16,128,128]{4,3,2,1,...) while((s32[]{:T(128)}, bf16[1,16,128,128]{3,2,1,0:T(8,128)(2,1)S(1)}, ...), condition=%wide.region_4.5_spmd.clone, body=%wide.region_3.4_spmd.clone.sunk | while | flops 1835032 | bytes 1573191 | solution.py:24
  163.4 1.5 fusion.69
  165.0 1.4 fusion.69
  166.4 1.4 fusion.69
  167.9 1.4 fusion.69
  169.4 1.4 fusion.69
  170.8 1.4 fusion.69
  172.3 1.4 fusion.69
  173.8 1.4 fusion.69
  175.2 0.5 fusion.9
  175.7 0.5 copy-done.12
  176.3 0.3 fusion.19
  176.6 0.5 convolution_bitcast_fusion.1
  177.0 0.5 copy-done.8
  177.5 1.2 fusion.4
  178.8 0.0 reduce-scatter.3.cloned.1.call-update
  178.8 0.0 reduce-scatter.5.cloned.1.call-start
  178.8 2.7 convolution_bitcast_fusion
  181.6 1.7 fusion.12
  183.3 1.0 copy.120
  184.3 17.8 %reduce-scatter.3.cloned.1.call-done = bf16[1024,128]{1,0:T(8,128)(2,1)} async-done(((bf16[4096,128]{1,0:T(8,128)(2,1)}), bf16[1024,128]{1,0:T(8,128)(2,1)}) %reduce-scatter.3.cloned.1.call-update) | async-done | bytes 262160 | tf_op jit(solution)/shard_map/reduce_scatter | solution.py:131
  202.1 0.0 reduce-scatter.5.cloned.1.call-update
  202.1 0.3 convolution_convert_fusion.1
  202.4 1.0 copy.118
  203.4 0.3 convolution_convert_fusion
  203.7 1.0 copy.119
  204.7 62.1 %reduce-scatter.5.cloned.1.call-done = bf16[128,128]{1,0:T(8,128)(2,1)} async-done(((bf16[1024,128]{1,0:T(8,128)(2,1)}), bf16[128,128]{1,0:T(8,128)(2,1)}) %reduce-scatter.5.cloned.1.call-update) | async-done | bytes 32784 | tf_op jit(solution)/shard_map/reduce_scatter | solution.py:134
  266.9 1.4 convert_element_type.228
  (45 shorter events, 0.2 us)
Async XLA Ops:
  7.2 6.8 %copy-start = (bf16[16,128,128]{2,1,0:T(8,128)(2,1)S(1)}, bf16[16,128,128]{2,1,0:T(8,128)(2,1)}, u32[]{:S(2)}) copy-start(bf16[16,128,128]{2,1,0:T(8,128)(2,1)} %param.16) | copy-start | bytes 1572868
  7.2 4.1 %copy-start.9 = (bf16[16,128,128]{2,1,0:T(8,128)(2,1)S(1)}, bf16[16,128,128]{2,1,0:T(8,128)(2,1)}, u32[]{:S(2)}) copy-start(bf16[16,128,128]{2,1,0:T(8,128)(2,1)} %param.17) | copy-start | bytes 1572868
  7.2 82.4 %all-gather.6.cloned.1.call-start = ((), (), s32[]{:S(2)}) async-start(), calls=%async_computation.4 | async-start | bytes 4718592 | tf_op jit(solution)/shard_map/all_gather | solution.py:11
  9.9 3.4 %copy-start.2 = (bf16[1,128,2048]{1,2,0:T(8,128)(2,1)}, bf16[1,128,2048]{1,2,0:T(8,128)(2,1)S(1)}, u32[]{:S(2)}) copy-start(bf16[1,128,2048]{1,2,0:T(8,128)(2,1)S(1)} %copy.132) | copy-start | bytes 1572868
  11.2 0.8 copy-start.4
  11.2 2.1 copy-start.13
  11.6 2.1 copy-start.14
  13.3 150.1 %all-gather.8.cloned.1.call-start = ((), (), s32[]{:S(2)}) async-start(), calls=%async_computation.5 | async-start | bytes 4718592 | tf_op jit(solution)/shard_map/all_gather | solution.py:11
  13.7 87.7 %copy-start.1 = (bf16[1,128,2048]{1,2,0:T(8,128)(2,1)}, bf16[1,128,2048]{1,2,0:T(8,128)(2,1)S(1)}, u32[]{:S(2)}) copy-start(bf16[1,128,2048]{1,2,0:T(8,128)(2,1)S(1)} %copy.133) | copy-start | bytes 1572868
  14.0 2.1 copy-start.6
  16.0 186.1 %reduce-scatter.3.cloned.1.call-start = ((), (), s32[]{:S(2)}) async-start(), calls=%async_computation.2 | async-start | bytes 1310720 | tf_op jit(solution)/shard_map/reduce_scatter | solution.py:131
  101.3 1.0 copy-start.11
  101.3 1.5 copy-start.7
  163.4 11.8 %copy-start.5 = (bf16[16,8,16,128]{3,2,1,0:T(8,128)(2,1)S(1)}, bf16[16,8,16,128]{3,2,1,0:T(8,128)(2,1)}, u32[]{:S(2)}) copy-start(bf16[16,8,16,128]{3,2,1,0:T(8,128)(2,1)} %copy-done.4) | copy-start | bytes 1572868
  175.2 1.0 copy-start.12
  175.2 1.3 copy-start.3
  176.2 1.3 copy-start.8
  178.8 88.1 %reduce-scatter.5.cloned.1.call-start = ((), (), s32[]{:S(2)}) async-start(), calls=%async_computation.3 | async-start | bytes 294912 | tf_op jit(solution)/shard_map/reduce_scatter | solution.py:134
  183.3 20.2 %copy-start.10 = (bf16[16,128,128]{2,1,0:T(8,128)(2,1)S(1)}, bf16[16,128,128]{2,1,0:T(8,128)(2,1)}, u32[]{:S(2)}) copy-start(bf16[16,128,128]{2,1,0:T(8,128)(2,1)} %param.17) | copy-start | bytes 1572868
Sparse Core Ops, SparseCore 0:
  13.5 76.1 all-gather.5
  91.7 71.6 all-gather.7
  178.9 23.1 reduce-scatter.2
  205.6 61.1 reduce-scatter.4
where the time goes:
time: 276 us; the launch traced here: 275 us
  waiting for transfers between devices  188 us (68%)
  other arithmetic  26.7 us (10%)
  blocking collectives  22.3 us (8%)
  matrix products  14.6 us (5%)
  between operations  14.1 us (5%)
  local copies, waits for them, and re-layouts  8.55 us (3%)
    all_gather x2, waiting for transfers between devices, carried_in(): everything = jax.tree.map(lambda part: lax.all_gather(part, axis), value)  108 us
    reduce_scatter x1, waiting for transfers between devices, per_device(): lax.psum_scatter(by_group, 'context', scatter_dimension=0, tiled=True)  62.1 us
    select_n x16, other arithmetic, hop(): return jax.tree.map(lambda a, b: jnp.where(reached, a, b), new, before)  22.8 us
    all_gather x1, blocking collectives, carried_in(): everything = jax.tree.map(lambda part: lax.all_gather(part, axis), value)  22.3 us
    reduce_scatter x1, waiting for transfers between devices, per_device(): lax.psum_scatter(partial_sums.astype(jnp.bfloat16), 'dp', scatter_dimensi...  17.8 us
    unnamed x35, local copies, waits for them, and re-layouts  6.62 us
  transfers between devices with their start and end apart: 4, of which 4 were waited for; matrix products, arithmetic and copies ran while one was open for 10% of the time, Pallas kernels for 0%

commit v1 on v0

v1 whole, which is shorter than its diff:
```python
import functools

import jax
import jax.numpy as jnp
from jax import lax
from jax.experimental import pallas as pl
from jax.experimental.pallas import tpu as pltpu
from jax.sharding import PartitionSpec as P

MESH = pl.DeviceIdType.MESH
BF16, F32 = jnp.bfloat16, jnp.float32


def nn(a, b):
    return lax.dot_general(a, b, (((1,), (0,)), ((), ())), preferred_element_type=F32)


def nt(a, b):
    return lax.dot_general(a, b, (((1,), (1,)), ((), ())), preferred_element_type=F32)


def tn(a, b):
    return lax.dot_general(a, b, (((0,), (0,)), ((), ())), preferred_element_type=F32)


def kernel(
    sizes, q_ref, k_ref, v_ref, o_ref, gate_ref, wq_ref, wk_ref,
    dq_ref, dk_ref, dv_ref, dm_ref,
    run, fq, fk, qt, kt, vt, xg, cl, zin, zout, pm, rc, sy, ry, a2, sz, rz, a3, sx, rx,
    c_send, c_recv, x_send, x_recv, z_send, z_recv,
    rc_send, rc_recv, ry_send, ry_recv, rz_send, rz_recv, rx_send, rx_recv,
):
    Y, Z, X, H, W, T, NG, HP, map_scale = sizes
    key_scale = W ** (-0.5) / 16.0
    dp, ctx = lax.axis_index("dp"), lax.axis_index("context")
    y, core = lax.div(dp, 2), lax.rem(dp, 2)
    z, x = lax.div(ctx, X), lax.rem(ctx, X)
    x_peer = lambda i: (dp, z * X + lax.rem(x + i, X))
    z_peer = lambda i: (dp, lax.rem(z + i, Z) * X + x)
    y_peer = lambda i: (lax.rem(y + i, Y) * 2 + core, ctx)
    core_peer = (y * 2 + 1 - core, ctx)

    peers = [x_peer(i) for i in range(1, X)] + [z_peer(i) for i in range(1, Z)]
    peers += [y_peer(i) for i in range(1, Y)] + [core_peer]
    barrier = pltpu.get_barrier_semaphore()
    for peer in peers:
        pl.semaphore_signal(barrier, inc=1, device_id=peer, device_id_type=MESH)

    def remote(src, dst, send, recv, peer):
        return pltpu.make_async_remote_copy(
            src_ref=src, dst_ref=dst, send_sem=send, recv_sem=recv,
            device_id=peer, device_id_type=MESH,
        )

    rows = lax.broadcasted_iota(jnp.int32, (T, T), 0)
    cols = lax.broadcasted_iota(jnp.int32, (T, T), 1)
    causal = rows >= cols

    upper = jnp.where(rows <= cols, 1.0, 0.0).astype(F32)
    run[...] = lax.dot_general(
        gate_ref[...], upper, (((1,), (0,)), ((), ())),
        precision=lax.Precision.HIGHEST, preferred_element_type=F32,
    )
    closing_rows = jnp.broadcast_to(run[:, T - 1 : T], (H, W))
    cl[x] = closing_rows.astype(BF16).astype(F32)
    pl.semaphore_wait(barrier, len(peers))

    def c_copy(i):
        return remote(cl.at[x], cl.at[x], c_send.at[i - 1], c_recv.at[i - 1], x_peer(i))

    def x_copy(i, g):
        return remote(
            xg.at[x, g], xg.at[x, g], x_send.at[i - 1, g], x_recv.at[i - 1, g], x_peer(i)
        )

    for i in range(1, X):
        c_copy(i).start()

    def columns(h):
        return pl.ds(pl.multiple_of(h * W, W), W)

    def tables(h):
        by_col = jnp.broadcast_to(run[pl.ds(h, 1), :], (T, T))
        by_row = by_col.T
        closing = by_row[T - 1 : T, :]
        return by_col, by_row, closing

    def local_states(g, carry):
        for hh in range(HP):
            h = g * HP + hh
            _, by_row, closing = tables(h)
            feat_q = nn(q_ref[:, columns(h)], wq_ref[h]).astype(BF16)
            feat_k = (nn(k_ref[:, columns(h)], wk_ref[h]) * key_scale).astype(BF16)
            fq[h] = feat_q
            fk[h] = feat_k
            end_w, start_w = jnp.exp(closing - by_row), jnp.exp(by_row)
            key_w = (feat_k.astype(F32) * end_w).astype(BF16)
            query_w = (feat_q.astype(F32) * start_w).astype(BF16)
            xg[x, g, 0, hh] = tn(key_w, v_ref[:, columns(h)]).astype(BF16)
            xg[x, g, 1, hh] = tn(query_w, o_ref[:, columns(h)]).astype(BF16)
        for i in range(1, X):
            x_copy(i, g).start()
        return carry

    lax.fori_loop(0, NG, local_states, 0)

    def within_block(g, carry):
        for hh in range(HP):
            h = g * HP + hh
            by_col, by_row, _ = tables(h)
            within = jnp.where(causal, jnp.exp(jnp.where(causal, by_row - by_col, 0.0)), 0.0)
            out, val = o_ref[:, columns(h)], v_ref[:, columns(h)]
            feat_q, feat_k = fq[h], fk[h]
            scores = (nt(feat_q, feat_k) * within).astype(BF16)
            grad_scores = (nt(out, val) * within).astype(BF16)
            qt[h] = nn(grad_scores, feat_k)
            kt[h] = tn(grad_scores, feat_q)
            vt[h] = tn(scores, out)
        return carry

    lax.fori_loop(0, NG, within_block, 0)
    for i in range(1, X):
        c_copy(i).wait_recv()

    def along(way, p):
        return p + way * (X - 1 - 2 * p)

    def decay(at, h):
        return jnp.exp(cl[at, pl.ds(h, 1), :])

    def z_copy(way, g):
        return remote(
            zout.at[way, g], zin.at[way, g], z_send.at[way, g], z_recv.at[way, g],
            (dp, (z + 1 - 2 * way) * X + x),
        )

    def ends(way):
        spot = z + way * (Z - 1 - 2 * z)
        return spot > 0, spot < Z - 1

    def chain(way, g):
        has_before, has_after = ends(way)

        @pl.when(has_before)
        def _():
            z_copy(way, g).wait_recv()

        @pl.when(jnp.logical_not(has_before))
        def _():
            zin[way, g] = jnp.zeros(zin.shape[2:], BF16)

        @pl.when(has_after)
        def _():
            for hh in range(HP):
                total = zin[way, g, hh].astype(F32)
                for p in range(X):
                    at = along(way, p)
                    total = total * decay(at, g * HP + hh) + xg[at, g, way, hh].astype(F32)
                zout[way, g, hh] = total.astype(BF16)
            z_copy(way, g).start()

    early_way = jnp.where(z < Z // 2, 0, 1)

    def early(g):
        for i in range(1, X):
            x_copy(i, g).wait_recv()
        chain(early_way, g)

    def carried(way, g, hh):
        spot = x + way * (X - 1 - 2 * x)
        total = zin[way, g, hh].astype(F32)
        for p in range(X - 1):
            at = along(way, p)
            joined = total * decay(at, g * HP + hh) + xg[at, g, way, hh].astype(F32)
            total = jnp.where(p < spot, joined, total)
        return total.astype(BF16)

    def finish(g):
        chain(1 - early_way, g)
        for hh in range(HP):
            h = g * HP + hh
            _, by_row, closing = tables(h)
            end_w, start_w = jnp.exp(closing - by_row), jnp.exp(by_row)
            state_in, grad_in = carried(0, g, hh), carried(1, g, hh)
            que, key = q_ref[:, columns(h)], k_ref[:, columns(h)]
            out, val = o_ref[:, columns(h)], v_ref[:, columns(h)]
            query_back = (qt[h] + nt(out, state_in) * start_w).astype(BF16)
            key_back = ((kt[h] + nt(val, grad_in) * end_w) * key_scale).astype(BF16)
            dv_ref[:, columns(h)] = (vt[h] + nn(fk[h], grad_in) * end_w).astype(BF16)
            dq_ref[:, columns(h)] = nt(query_back, wq_ref[h]).astype(BF16)
            dk_ref[:, columns(h)] = nt(key_back, wk_ref[h]).astype(BF16)
            pm[columns(h), :] = (tn(que, query_back) * map_scale).astype(BF16)
            pm[columns(H + h), :] = (tn(key, key_back) * map_scale).astype(BF16)

    early(0)

    def step(g, carry):
        early(g)
        finish(g - 1)
        return carry

    lax.fori_loop(1, NG, step, 0)
    finish(NG - 1)

    per_y = a2.shape[0]
    per_z, own = a3.shape[0], dm_ref.shape[0]

    def part(yy, cc):
        return pl.ds(pl.multiple_of((yy * 2 + cc) * per_y, per_y), per_y)

    core_copies = [
        remote(pm.at[part(yy, 1 - core)], rc.at[yy], rc_send.at[yy], rc_recv.at[yy], core_peer)
        for yy in range(Y)
    ]
    y_copies = [
        remote(sy.at[i - 1], ry.at[i - 1], ry_send.at[i - 1], ry_recv.at[i - 1], y_peer(i))
        for i in range(1, Y)
    ]
    z_copies = [
        remote(sz.at[i - 1], rz.at[i - 1], rz_send.at[i - 1], rz_recv.at[i - 1], z_peer(i))
        for i in range(1, Z)
    ]
    x_copies = [
        remote(sx.at[i - 1], rx.at[i - 1], rx_send.at[i - 1], rx_recv.at[i - 1], x_peer(i))
        for i in range(1, X)
    ]
    for copy in core_copies:
        copy.start()
    for copy in core_copies:
        copy.wait_recv()
    for i in range(1, Y):
        yt = lax.rem(y + i, Y)
        sy[i - 1] = (pm[part(yt, core), :].astype(F32) + rc[yt].astype(F32)).astype(BF16)
        y_copies[i - 1].start()
    a2[...] = pm[part(y, core), :].astype(F32) + rc[y].astype(F32)
    for i in range(1, Y):
        y_copies[i - 1].wait_recv()
        a2[...] += ry[i - 1].astype(F32)
    for i in range(1, Z):
        zt = lax.rem(z + i, Z)
        sz[i - 1] = a2[pl.ds(pl.multiple_of(zt * per_z, per_z), per_z), :].astype(BF16)
        z_copies[i - 1].start()
    a3[...] = a2[pl.ds(pl.multiple_of(z * per_z, per_z), per_z), :]
    for i in range(1, Z):
        z_copies[i - 1].wait_recv()
        a3[...] += rz[i - 1].astype(F32)
    for i in range(1, X):
        xt = lax.rem(x + i, X)
        sx[i - 1] = a3[pl.ds(pl.multiple_of(xt * own, own), own), :].astype(sx.dtype)
        x_copies[i - 1].start()
    total = a3[pl.ds(pl.multiple_of(x * own, own), own), :]
    for i in range(1, X):
        x_copies[i - 1].wait_recv()
        total = total + rx[i - 1].astype(F32)
    dm_ref[...] = total

    for copy in core_copies + y_copies + z_copies + x_copies:
        copy.wait_send()
    for i in range(1, X):
        c_copy(i).wait_send()
    for way in range(2):
        @pl.when(ends(way)[1])
        def _():
            for g in range(NG):
                z_copy(way, g).wait_send()
    for g in range(NG):
        for i in range(1, X):
            x_copy(i, g).wait_send()


def solution(mesh):
    n_dp, n_ctx = mesh.shape["dp"], mesh.shape["context"]
    X = 1
    while 2 * (2 * X) ** 2 <= n_ctx:
        X *= 2
    Z, Y = n_ctx // X, n_dp // 2

    def per_device(queries, keys, values, out_grad, log_gates, query_map, key_map):
        H, W = query_map.shape[:2]
        T = queries.shape[1]
        NG = 4
        HP = H // NG
        own = 2 * H * W // (n_dp * n_ctx)
        map_scale = float(T * n_ctx * n_dp * queries.shape[0]) ** (-0.5)
        sizes = (Y, Z, X, H, W, T, NG, HP, map_scale)
        per_y, per_z = own * X * Z, own * X
        last = BF16 if own % 16 == 0 else F32
        dma = pltpu.SemaphoreType.DMA
        vmem = pl.BlockSpec(memory_space=pltpu.VMEM)
        grads = pl.pallas_call(
            functools.partial(kernel, sizes),
            out_shape=[jax.ShapeDtypeStruct((T, H * W), BF16)] * 3
            + [jax.ShapeDtypeStruct((own, W), F32)],
            in_specs=[vmem] * 7,
            out_specs=[vmem] * 4,
            scratch_shapes=[
                pltpu.VMEM((H, T), F32),
                pltpu.VMEM((H, T, W), BF16),
                pltpu.VMEM((H, T, W), BF16),
                pltpu.VMEM((H, T, W), F32),
                pltpu.VMEM((H, T, W), F32),
                pltpu.VMEM((H, T, W), F32),
                pltpu.VMEM((X, NG, 2, HP, W, W), BF16),
                pltpu.VMEM((X, H, W), F32),
                pltpu.VMEM((2, NG, HP, W, W), BF16),
                pltpu.VMEM((2, NG, HP, W, W), BF16),
                pltpu.VMEM((2 * H * W, W), BF16),
                pltpu.VMEM((Y, per_y, W), BF16),
                pltpu.VMEM((Y - 1, per_y, W), BF16),
                pltpu.VMEM((Y - 1, per_y, W), BF16),
                pltpu.VMEM((per_y, W), F32),
                pltpu.VMEM((Z - 1, per_z, W), BF16),
                pltpu.VMEM((Z - 1, per_z, W), BF16),
                pltpu.VMEM((per_z, W), F32),
                pltpu.VMEM((X - 1, own, W), last),
                pltpu.VMEM((X - 1, own, W), last),
                dma((X - 1,)), dma((X - 1,)),
                dma((X - 1, NG)), dma((X - 1, NG)),
                dma((2, NG)), dma((2, NG)),
                dma((Y,)), dma((Y,)),
                dma((Y - 1,)), dma((Y - 1,)),
                dma((Z - 1,)), dma((Z - 1,)),
                dma((X - 1,)), dma((X - 1,)),
            ],
            compiler_params=pltpu.CompilerParams(
                collective_id=0, has_side_effects=True, vmem_limit_bytes=48 * 1024 * 1024
            ),
        )(queries[0], keys[0], values[0], out_grad[0], log_gates[0], query_map, key_map)
        return grads[0][None], grads[1][None], grads[2][None], grads[3]

    return jax.shard_map(
        per_device,
        mesh=mesh,
        in_specs=(
            P("dp", "context", None),
            P("dp", "context", None),
            P("dp", "context", None),
            P("dp", "context", None),
            P("dp", None, "context"),
            P(),
            P(),
        ),
        out_specs=(
            P("dp", "context", None),
            P("dp", "context", None),
            P("dp", "context", None),
            P(("dp", "context"), None),
        ),
        check_vma=False,
    )
```

time: 276 us -> 77.2 us (0.28)
  waiting for transfers between devices: 188 us -> 0 us
  Pallas kernels: 0 us -> 66.2 us
  other arithmetic: 26.7 us -> 0 us
  blocking collectives: 22.3 us -> 0 us
  matrix products: 14.6 us -> 0 us
  between operations: 14.1 us -> 0.66 us
    all_gather x2 -> x0, waiting for transfers between devices: 108 us -> none  [carried_in(): everything = jax.tree.map(lambda part: lax.all_gather(part, axis), value)]
    reduce_scatter x2 -> x0, waiting for transfers between devices: 79.9 us -> none  [the longest x1 62.1 us: per_device(): lax.psum_scatter(by_group, 'context', scatter_dimension=0, tiled=True)]
    pallas_call x0 -> x1, Pallas kernels: none -> 66.2 us  [per_device(): pl.pallas_call(functools.partial(kernel, sizes), out_shape=[jax.ShapeDtyp...]
    select_n x16 -> x0, other arithmetic: 22.8 us -> none  [hop(): return jax.tree.map(lambda a, b: jnp.where(reached, a, b), new, before)]
    all_gather x1 -> x0, blocking collectives: 22.3 us -> none  [carried_in(): everything = jax.tree.map(lambda part: lax.all_gather(part, axis), value)]
    dot_general x15 -> x0, matrix products: 14.6 us -> none  [the longest x1 2.72 us: per_device(): jnp.einsum('bhts,bthd->bshd', scores, grad_heads, preferred_element_type=...]
    unnamed x35 -> x18, local copies, waits for them, and re-layouts: 6.62 us -> 9.95 us
  transfers between devices with their start and end apart: 4 -> 0, of which waited for: 4 -> 0; matrix products, arithmetic and copies ran while one was open for 10% -> 0% of each run, Pallas kernels for 0% -> 0%
where the time goes in v1:
time: 77.2 us; the launch traced here: 76.8 us
  Pallas kernels  66.2 us (86%)
  local copies, waits for them, and re-layouts  9.95 us (13%)
    pallas_call x1, Pallas kernels, per_device(): pl.pallas_call(functools.partial(kernel, sizes), out_shape=[jax.ShapeDtyp...  66.2 us
    unnamed x18, local copies, waits for them, and re-layouts  9.95 us

profile of v1, /device:TPU:0, one launch (start us, length us, event | category | flops | bytes accessed | tf_op | source)
XLA Modules:
  0.0 76.8 jit_solution(10299184220719099475)
XLA Ops:
  0.6 0.0 copy-start.6
  0.6 0.7 copy-done.6
  1.3 0.0 copy-start
  1.3 1.0 %copy-done = bf16[1,128,2048]{2,1,0:T(8,128)(2,1)S(1)} copy-done((bf16[1,128,2048]{2,1,0:T(8,128)(2,1)S(1)}, bf16[1,128,2048]{2,1,0:T(8,128)(2,1)}, u32[]{:S(2)}) %copy-start) | copy-done | bytes 524312
  2.4 0.0 copy-start.1
  2.4 1.0 %copy-done.1 = bf16[1,128,2048]{2,1,0:T(8,128)(2,1)S(1)} copy-done((bf16[1,128,2048]{2,1,0:T(8,128)(2,1)S(1)}, bf16[1,128,2048]{2,1,0:T(8,128)(2,1)}, u32[]{:S(2)}) %copy-start.1) | copy-done | bytes 524312
  3.4 0.0 copy-start.2
  3.4 1.0 %copy-done.2 = bf16[1,128,2048]{2,1,0:T(8,128)(2,1)S(1)} copy-done((bf16[1,128,2048]{2,1,0:T(8,128)(2,1)S(1)}, bf16[1,128,2048]{2,1,0:T(8,128)(2,1)}, u32[]{:S(2)}) %copy-start.2) | copy-done | bytes 524312
  4.5 0.0 copy-start.3
  4.5 1.0 %copy-done.3 = bf16[1,128,2048]{2,1,0:T(8,128)(2,1)S(1)} copy-done((bf16[1,128,2048]{2,1,0:T(8,128)(2,1)S(1)}, bf16[1,128,2048]{2,1,0:T(8,128)(2,1)}, u32[]{:S(2)}) %copy-start.3) | copy-done | bytes 524312
  5.5 0.0 copy-start.4
  5.5 1.0 %copy-done.4 = bf16[16,128,128]{2,1,0:T(8,128)(2,1)S(1)} copy-done((bf16[16,128,128]{2,1,0:T(8,128)(2,1)S(1)}, bf16[16,128,128]{2,1,0:T(8,128)(2,1)}, u32[]{:S(2)}) %copy-start.4) | copy-done | bytes 524312
  6.5 0.0 copy-start.5
  6.5 1.0 %copy-done.5 = bf16[16,128,128]{2,1,0:T(8,128)(2,1)S(1)} copy-done((bf16[16,128,128]{2,1,0:T(8,128)(2,1)S(1)}, bf16[16,128,128]{2,1,0:T(8,128)(2,1)}, u32[]{:S(2)}) %copy-start.5) | copy-done | bytes 524312
  7.6 66.2 %shard_map.102 = (bf16[128,2048]{1,0:T(8,128)(2,1)S(1)}, bf16[128,2048]{1,0:T(8,128)(2,1)S(1)}, bf16[128,2048]{1,0:T(8,128)(2,1)S(1)}, f32[128,128]{1,0:T(8,128)S(1)}) custom-call(bf16[128,2048]{1,0:T(8,128)(2,1)S(1)} %bitcast.11, bf16[128,2048]{1,0:T(8,128)(2,1)S(1)} %bitcast.12, bf16[128,2048]{1,0:T(8,128)(2,1)S(1)} %bitcast.13, ...), custom_call_target="tpu_custom_call" | custom-call | tf_op jit(solution)/shard_map/pallas_call | solution.py:290
  73.8 0.8 %copy.15 = bf16[1,128,2048]{2,1,0:T(8,128)(2,1)} copy(bf16[1,128,2048]{2,1,0:T(8,128)(2,1)S(1)} %bitcast.10) | data formatting | bytes 1048576
  74.6 0.8 %copy.16 = bf16[1,128,2048]{2,1,0:T(8,128)(2,1)} copy(bf16[1,128,2048]{2,1,0:T(8,128)(2,1)S(1)} %bitcast.9) | data formatting | bytes 1048576
  75.4 0.8 %copy.17 = bf16[1,128,2048]{2,1,0:T(8,128)(2,1)} copy(bf16[1,128,2048]{2,1,0:T(8,128)(2,1)S(1)} %bitcast.8) | data formatting | bytes 1048576
  76.1 0.6 copy.18
Async XLA Ops:
  0.6 0.7 copy-start.6
  1.3 1.0 %copy-start = (bf16[1,128,2048]{2,1,0:T(8,128)(2,1)S(1)}, bf16[1,128,2048]{2,1,0:T(8,128)(2,1)}, u32[]{:S(2)}) copy-start(bf16[1,128,2048]{2,1,0:T(8,128)(2,1)} %param.7) | copy-start | bytes 1572868
  2.4 1.0 %copy-start.1 = (bf16[1,128,2048]{2,1,0:T(8,128)(2,1)S(1)}, bf16[1,128,2048]{2,1,0:T(8,128)(2,1)}, u32[]{:S(2)}) copy-start(bf16[1,128,2048]{2,1,0:T(8,128)(2,1)} %param.8) | copy-start | bytes 1572868
  3.4 1.0 %copy-start.2 = (bf16[1,128,2048]{2,1,0:T(8,128)(2,1)S(1)}, bf16[1,128,2048]{2,1,0:T(8,128)(2,1)}, u32[]{:S(2)}) copy-start(bf16[1,128,2048]{2,1,0:T(8,128)(2,1)} %param.9) | copy-start | bytes 1572868
  4.5 1.0 %copy-start.3 = (bf16[1,128,2048]{2,1,0:T(8,128)(2,1)S(1)}, bf16[1,128,2048]{2,1,0:T(8,128)(2,1)}, u32[]{:S(2)}) copy-start(bf16[1,128,2048]{2,1,0:T(8,128)(2,1)} %param.10) | copy-start | bytes 1572868
  5.5 1.0 %copy-start.4 = (bf16[16,128,128]{2,1,0:T(8,128)(2,1)S(1)}, bf16[16,128,128]{2,1,0:T(8,128)(2,1)}, u32[]{:S(2)}) copy-start(bf16[16,128,128]{2,1,0:T(8,128)(2,1)} %wq_ref.1) | copy-start | bytes 1572868
  6.5 1.0 %copy-start.5 = (bf16[16,128,128]{2,1,0:T(8,128)(2,1)S(1)}, bf16[16,128,128]{2,1,0:T(8,128)(2,1)}, u32[]{:S(2)}) copy-start(bf16[16,128,128]{2,1,0:T(8,128)(2,1)} %wk_ref.1) | copy-start | bytes 1572868
